TPU v7x, 32 devices: a whole 2x2x4 slice. The times are simulated.
32 devices in a mesh: parts: 2 (over y), term: 4 (over z), blk: 4 (over x, core).
Axes of the slice: x: 2, y: 2, z: 4, core: 2. Of those that a mesh axis runs over, the one named last changes fastest.
Arguments:
- wavefunction: bfloat16 [8, 384, 384], P('parts', 'term'), parts along dimension 0
- left_operator_table: bfloat16 [64, 3, 384, 384], P(('parts', 'term', 'blk')), parts along dimension 0
- op_right: bfloat16 [64, 3, 384, 384], P(('parts', 'term', 'blk')), parts along dimension 0
- term_source: int32 [64, 3], P(('parts', 'term', 'blk')), parts along dimension 0, may hold values from 0 to 3, as said below
- term_target: int32 [64, 3], P(('parts', 'term', 'blk')), parts along dimension 0, may hold values from 0 to 3, as said below
Outputs:
- applied: float32 [8, 384, 384], P('parts', 'term'), parts along dimension 0
- residual: float32 [8, 384, 384], P('parts', 'term'), parts along dimension 0
There are 2 independent parts, one for each index of `parts`. A program takes and returns all parts, laid end to end along the dimension named above; each array names one. Nothing has to cross between parts.
Inputs may be any that keep to these rules, and one draw needn't show every extreme that they name: Each term has one shift q in -1, 0, 1; term_target = term_source + q; the 3 sources of a term are distinct and increasing, and all targets are sectors. term_target[t,k] = term_source[t,k] + q of term t, the same q for all slots of a term.
All inputs are finite; a program needn't handle non-finite values.
Results may differ from a plain program's by a relative error of at most 0.0031.
Values may be sent and summed in bfloat16 or wider, within the bound.
A program may use at most 64 MiB of HBM per device.

v0:
```python
import jax
import jax.numpy as jnp
from jax import lax
from jax.sharding import PartitionSpec as P


def local(wavefunction, left_operator_table, op_right, term_source, term_target):
    sectors = wavefunction.shape[0]
    block_width = wavefunction.shape[2]
    item_count = left_operator_table.shape[0] * left_operator_table.shape[1]
    left_operator_blocks = left_operator_table.reshape(item_count, block_width, block_width)
    right_blocks = op_right.reshape(item_count, block_width, block_width)
    source = term_source.reshape(item_count)
    target = term_target.reshape(item_count)
    whole_psi = lax.all_gather(wavefunction, "term", axis=1, tiled=True)
    selected_blocks = jnp.take(whole_psi, source, axis=0)
    half_products = jnp.einsum(
        "xwm,xmp->xwp", left_operator_blocks, selected_blocks, preferred_element_type=jnp.float32
    )
    half_products = half_products.astype(jnp.bfloat16)
    term_products = jnp.einsum(
        "iab,icb->iac", half_products, right_blocks, preferred_element_type=jnp.float32
    )
    onehot = (target[:, None] == jnp.arange(sectors, dtype=jnp.int32)[None, :]).astype(jnp.float32)
    partial_value = jnp.einsum(
        "is,iac->sac", onehot, term_products, precision=lax.Precision.HIGHEST
    )
    column_share = lax.psum_scatter(partial_value, "blk", scatter_dimension=2, tiled=True)
    both_share = lax.psum_scatter(column_share, "term", scatter_dimension=1, tiled=True)
    applied = lax.all_gather(both_share, "blk", axis=2, tiled=True)
    wave_float = wavefunction.astype(jnp.float32)
    correlation, norm_squared = lax.psum(
        (jnp.sum(wave_float * applied), jnp.sum(wave_float * wave_float)), "term"
    )
    rayleigh = correlation / (norm_squared + 1e-06)
    residual = applied - rayleigh * wave_float
    return (applied, residual)


def solution(mesh):
    return jax.shard_map(
        local,
        mesh=mesh,
        in_specs=(
            P("parts", "term", None),
            P(("parts", "term", "blk"), None, None, None),
            P(("parts", "term", "blk"), None, None, None),
            P(("parts", "term", "blk"), None),
            P(("parts", "term", "blk"), None),
        ),
        out_specs=(P("parts", "term", None), P("parts", "term", None)),
        check_vma=False,
    )
```

profile of v0, /device:TPU:1, one launch (start us, length us, event | category | flops | bytes accessed | tf_op | source)
XLA Modules:
  0.0 195.2 jit_solution(12800012337169962332)
XLA Ops:
  7.2 0.0 copy-start
  7.2 0.0 all-gather.2.cloned.1.call-start
  7.2 0.7 all-gather.2.cloned.1.call-update
  7.9 0.0 all-reduce.6.cloned.1.call-start
  8.0 0.8 reshape.51
  8.7 0.8 reshape.50
  9.5 0.8 eq.15
  10.3 31.3 %all-gather.2.cloned.1.call-done = bf16[4,384,384]{2,1,0:T(8,128)(2,1)} async-done(((bf16[4,96,384]{2,1,0:T(8,128)(2,1)}), bf16[4,384,384]{2,1,0:T(8,128)(2,1)}) %all-gather.2.cloned.1.call-update) | async-done | bytes 1179664 | tf_op jit(solution)/shard_map/all_gather | solution.py:15
  41.6 2.2 %gather_fusion = bf16[6,384,384]{2,1,0:T(8,128)(2,1)S(1)} fusion(bf16[4,384,384]{2,1,0:T(8,128)(2,1)} %all-gather.2.cloned.1.call-done, s32[1024]{0:T(1024)S(1)} %pad_clamp_fusion), kind=kCustom, calls=%fused_computation | custom fusion | bytes 3538968 | tf_op jit(solution)/shard_map/jit(_take)/gather | solution.py:16
  43.8 0.0 copy-done
  43.8 5.9 %fusion = f32[6,384,384]{2,1,0:T(8,128)} fusion(bf16[6,384,384]{2,1,0:T(8,128)(2,1)S(1)} %bitcast.15, bf16[6,384,384]{2,1,0:T(8,128)(2,1)} %bitcast.19, bf16[6,384,384]{2,1,0:T(8,128)(2,1)S(1)} %gather_fusion, pred[6]{0:T(512)(128)(4,1)S(1)} %compare_and_fusion), kind=kOutput, calls=%fused_computation.1 | convolution fusion | flops 1360723968 | bytes 8847366 | tf_op jit(solution)/shard_map/iab,icb->iac/dot_general | solution.py:21
  49.7 5.6 %copy.17 = f32[6,384,384]{1,0,2:T(8,128)} copy(f32[6,384,384]{2,1,0:T(8,128)} %fusion) | data formatting | bytes 7077888 | tf_op jit(solution)/shard_map/iab,icb->iac/dot_general | solution.py:21
  55.3 6.1 %fusion.14 = f32[4,384,384]{1,0,2:T(4,128)} fusion(f32[6,384,384]{1,0,2:T(8,128)} %copy.17, s32[6]{0:T(128)S(1)} %eq.15), kind=kOutput, calls=%fused_computation.18 | convolution fusion | flops 42467352 | bytes 5898264 | tf_op jit(solution)/shard_map/is,iac->sac/dot_general | solution.py:25
  61.4 0.0 copy-start.3
  61.4 0.0 all-reduce.6.cloned.1.call-update
  61.4 0.0 copy-start.1
  61.4 0.0 all-reduce.8.cloned.1.call-start
  61.5 0.6 copy-done.3
  62.0 0.6 dynamic-slice
  63.3 0.0 copy-start.2
  63.3 53.5 %all-reduce.6.cloned.1.call-done = f32[4,384,384]{1,0,2:T(4,128)} async-done(((f32[4,384,384]{1,0,2:T(4,128)}), f32[4,384,384]{1,0,2:T(4,128)}) %all-reduce.6.cloned.1.call-update) | async-done | bytes 2359312
  116.8 1.1 constant_dynamic-slice_fusion.1
  117.9 1.2 copy.11
  119.1 0.0 all-reduce.8.cloned.1.call-update
  119.1 0.0 copy-done.1
  119.2 0.2 copy.13
  119.4 0.0 copy-done.2
  119.4 0.6 dynamic-slice.2
  120.7 42.4 %all-reduce.8.cloned.1.call-done = f32[4,384,96]{2,0,1:T(4,128)} async-done(((f32[4,384,96]{2,0,1:T(4,128)}), f32[4,384,96]{2,0,1:T(4,128)}) %all-reduce.8.cloned.1.call-update) | async-done | bytes 589840
  163.0 0.9 constant_dynamic-slice_fusion
  164.0 0.1 copy.12
  164.1 9.2 %all_gather.7 = f32[4,96,384]{1,0,2:T(4,128)S(1)} all-gather(f32[4,96,96]{1,0,2:T(4,128)S(1)} %copy.12), channel_id=1, replica_groups=mesh['parts'=2,'term'=4,'blk'=4] {'blk'}, dimensions={2}, use_global_device_ids=true | all-gather | bytes 737280 | tf_op jit(solution)/shard_map/all_gather | solution.py:30
  173.3 1.1 copy.14
  174.4 1.1 fusion.11
  175.5 8.7 %all-reduce.2 = (f32[]{:T(128)}, f32[]{:T(128)}) all-reduce(f32[]{:T(128)} %get-tuple-element.7, f32[]{:T(128)} %get-tuple-element.6), channel_id=1, replica_groups=mesh['parts'=2,'term'=4,'blk'=4] {'term'}, use_global_device_ids=true, to_apply=%region_3.4 | all-reduce | flops 2 | bytes 16 | tf_op jit(solution)/shard_map/psum | solution.py:32
  185.5 1.0 fusion.12
  186.5 2.2 %copy.15 = f32[4,96,384]{2,1,0:T(8,128)} copy(f32[4,96,384]{1,0,2:T(4,128)} %bitcast.18) | data formatting | bytes 1179648
  (3 shorter events, 0.0 us)
Async XLA Ops:
  7.2 36.6 %copy-start = (bf16[2,3,384,384]{3,2,1,0:T(8,128)(2,1)S(1)}, bf16[2,3,384,384]{3,2,1,0:T(8,128)(2,1)}, u32[]{:S(2)}) copy-start(bf16[2,3,384,384]{3,2,1,0:T(8,128)(2,1)} %param.7) | copy-start | bytes 5308420
  7.2 34.4 %all-gather.2.cloned.1.call-start = ((), (), s32[]{:S(2)}) async-start(), calls=%async_computation | async-start | bytes 1474560 | tf_op jit(solution)/shard_map/all_gather | solution.py:15
  7.9 108.9 %all-reduce.6.cloned.1.call-start = ((), (), s32[]{:S(2)}) async-start(), calls=%async_computation.1 | async-start | bytes 4718592
  61.4 0.7 copy-start.3
  61.4 57.8 %copy-start.1 = (bf16[4,96,384]{2,1,0:T(8,128)(2,1)S(1)}, bf16[4,96,384]{2,1,0:T(8,128)(2,1)}, u32[]{:S(2)}) copy-start(bf16[4,96,384]{2,1,0:T(8,128)(2,1)} %param.5) | copy-start | bytes 884740
  61.4 101.6 %all-reduce.8.cloned.1.call-start = ((), (), s32[]{:S(2)}) async-start(), calls=%async_computation.2 | async-start | bytes 1572864
  63.3 56.2 %copy-start.2 = (u32[32]{0:T(128)S(1)}, u32[32]{0:T(128)}, u32[]{:S(2)}) copy-start(u32[32]{0:T(128)} %constant.30) | copy-start | bytes 388
Sparse Core Ops, SparseCore 0:
  9.6 31.9 all-gather.1
  61.5 55.2 all-reduce.5
  119.3 43.7 all-reduce.7
where the time goes:
time: 198 us; the launch traced here: 195 us
  waiting for transfers between devices  128 us (65%)
  local copies, waits for them, and re-layouts  18.8 us (9%)
  blocking collectives  17.9 us (9%)
  between operations  16.4 us (8%)
  matrix products  12 us (6%)
  other arithmetic  2.13 us (1%)
    unnamed x5, waiting for transfers between devices  96.6 us
    all_gather x1, waiting for transfers between devices, local(): whole_psi = lax.all_gather(wavefunction, 'term', axis=1, tiled=True)  31.3 us
    all_gather x1, blocking collectives, local(): applied = lax.all_gather(both_share, 'blk', axis=2, tiled=True)  9.17 us
    psum x1, blocking collectives, local(): lax.psum((jnp.sum(wave_float * applied), jnp.sum(wave_float * wave_float)...  8.72 us
    unnamed x15, local copies, waits for them, and re-layouts  7.37 us
    dot_general x1, matrix products, local(): jnp.einsum('is,iac->sac', onehot, term_products, precision=lax.Precision....  6.07 us
    dot_general x1, matrix products, local(): jnp.einsum('iab,icb->iac', half_products, right_blocks, preferred_element...  5.9 us
    dot_general x1, local copies, waits for them, and re-layouts, local(): jnp.einsum('iab,icb->iac', half_products, right_blocks, preferred_element...  5.59 us
  transfers between devices with their start and end apart: 3, of which 3 were waited for; matrix products, arithmetic and copies ran while one was open for 2% of the time, Pallas kernels for 0%

commit v1 on v0

v1 whole, which is shorter than its diff:
```python
import functools

import jax
import jax.numpy as jnp
from jax import lax
from jax.experimental import pallas as pl
from jax.experimental.pallas import tpu as pltpu
from jax.sharding import PartitionSpec as P

MESH = pl.DeviceIdType.MESH
F32 = jnp.float32
BF16 = jnp.bfloat16


def fold(product):
    rows, columns = product.shape
    return jnp.sum(product.reshape(rows // 8, 8, columns), axis=0)


def kernel(
    n, psi_ref, left_hbm, right_hbm, source_ref, target_ref,
    out_ref, rayleigh_ref,
    psi_all, left, right, half, kept, pair_send, pair_recv, x_send, x_recv, z_send, z_recv,
    own_block, dots, dots_recv,
    load_sem, gz_s, gz_r, gx_s, gx_r, gc_s, gc_r, gd_s, gd_r,
    pair_s, pair_r, x_s, x_r, z_s, z_r, out_s, out_r, dot_s, dot_r,
):
    terms, slots = left.shape[0], left.shape[1]
    rows = psi_ref.shape[1]
    me = lax.axis_index("term")
    blk = lax.axis_index("blk")
    core = lax.rem(blk, 2)
    x = lax.div(blk, 2)
    sib = blk + 1 - 2 * core
    across = blk + 2 - 4 * x
    diagonal = across + 1 - 2 * core

    loads = []
    for t in range(terms):
        loads.append(pltpu.make_async_copy(left_hbm.at[t], left.at[t], load_sem.at[0, t]))
        loads.append(pltpu.make_async_copy(right_hbm.at[t], right.at[t], load_sem.at[1, t]))
    for load in loads:
        load.start()

    def near(i):
        low = i + jnp.where(me <= i, 1, 0)
        high = n - 1 - (i + jnp.where(n - 1 - me <= i, 1, 0))
        return jnp.where(2 * me < n, low, high)

    peers = [near(i) for i in range(n - 1)]

    barrier = pltpu.get_barrier_semaphore()
    for peer in peers:
        pl.semaphore_signal(barrier, inc=1, device_id={"term": peer}, device_id_type=MESH)
    for peer in (sib, across, diagonal):
        pl.semaphore_signal(barrier, inc=1, device_id={"blk": peer}, device_id_type=MESH)
    pl.semaphore_wait(barrier, n - 1 + 3)

    sends = []

    def remote(src, dst, send, recv, where):
        return pltpu.make_async_remote_copy(
            src_ref=src, dst_ref=dst, send_sem=send, recv_sem=recv, device_id=where, device_id_type=MESH
        )

    def push(src, dst, send, recv, where):
        copy = remote(src, dst, send, recv, where)
        copy.start()
        sends.append(copy)

    def arrive(dst, send, recv, where):
        remote(dst, dst, send, recv, where).wait_recv()

    def span(z):
        return pl.ds(pl.multiple_of(z * rows, rows), rows)

    for peer in peers:
        push(psi_ref.at[blk], psi_all.at[blk, span(me)], gz_s.at[peer], gz_r.at[me], {"term": peer})
    for s in range(psi_ref.shape[0]):
        psi_all[s, span(me)] = psi_ref[s]

    for peer in peers:
        piece = psi_all.at[blk, span(peer)]
        arrive(piece, gz_s.at[peer], gz_r.at[peer], {"term": peer})
        push(piece, piece, gx_s.at[peer], gx_r.at[peer], {"blk": across})
        push(piece, piece, gc_s.at[peer], gc_r.at[peer], {"blk": sib})
    for peer in peers:
        piece = psi_all.at[across, span(peer)]
        arrive(piece, gx_s.at[peer], gx_r.at[peer], {"blk": across})
        push(piece, piece, gd_s.at[peer], gd_r.at[peer], {"blk": sib})
    for t in range(terms):
        half[t, slots] = jnp.zeros(half.shape[2:], BF16)
    for load in loads:
        load.wait()
    for peer in peers:
        arrive(psi_all.at[sib, span(peer)], gc_s.at[peer], gc_r.at[peer], {"blk": sib})
        arrive(psi_all.at[diagonal, span(peer)], gd_s.at[peer], gd_r.at[peer], {"blk": sib})

    for t in range(terms):
        for k in range(slots):
            half[t, k] = jnp.dot(
                left[t, k], psi_all[source_ref[t, k]], preferred_element_type=F32
            ).astype(BF16)

    def partial(s):
        total = None
        for t in range(terms):
            k = slots
            for slot in range(slots):
                k = jnp.where(target_ref[t, slot] == s, slot, k)
            product = lax.dot_general(
                half[t, k], right[t, jnp.minimum(k, slots - 1)],
                (((1,), (1,)), ((), ())), preferred_element_type=F32,
            )
            total = product if total is None else total + product
        return total, fold(psi_all[s].astype(F32) * total)

    far = peers[::-1]
    order = far + [me]

    value, dot = partial(diagonal)
    pair_send[0] = value.astype(BF16)
    push(pair_send.at[0], pair_recv.at[0], pair_s.at[0], pair_r.at[0], {"blk": sib})
    value, more = partial(across)
    dot = dot + more
    kept[0] = value
    arrive(pair_recv.at[0], pair_s.at[0], pair_r.at[0], {"blk": sib})
    for z in order:
        x_send[span(z)] = (kept[0, span(z)] + pair_recv[0, span(z)].astype(F32)).astype(BF16)
        push(x_send.at[span(z)], x_recv.at[span(z)], x_s.at[z], x_r.at[z], {"blk": across})
    value, more = partial(sib)
    dot = dot + more
    pair_send[1] = value.astype(BF16)
    push(pair_send.at[1], pair_recv.at[1], pair_s.at[1], pair_r.at[1], {"blk": sib})
    value, more = partial(blk)
    dots[0] = dot + more
    push(dots.at[0], dots_recv.at[0], dot_s.at[0], dot_r.at[0], {"blk": sib})
    kept[1] = value
    arrive(pair_recv.at[1], pair_s.at[1], pair_r.at[1], {"blk": sib})

    for i, z in enumerate(order):
        arrive(x_recv.at[span(z)], x_s.at[z], x_r.at[z], {"blk": across})
        block = (kept[1, span(z)] + pair_recv[1, span(z)].astype(F32)) + x_recv[span(z)].astype(F32)
        if i < n - 1:
            z_send[i] = block.astype(BF16)
            push(z_send.at[i], z_recv.at[me], z_s.at[z], z_r.at[me], {"term": z})
        else:
            own_block[...] = block
        if i == 0:
            arrive(dots_recv.at[0], dot_s.at[0], dot_r.at[0], {"blk": sib})
            dots[1] = dots[0] + dots_recv[0]
            push(dots.at[1], dots_recv.at[1], dot_s.at[1], dot_r.at[1], {"blk": across})
        if i == 2:
            arrive(dots_recv.at[1], dot_s.at[1], dot_r.at[1], {"blk": across})
            dots[2] = dots[1] + dots_recv[1]
            for peer in peers:
                push(dots.at[2], dots_recv.at[2 + me], dot_s.at[2 + peer], dot_r.at[2 + me], {"term": peer})

    norm = None
    for s in range(psi_ref.shape[0]):
        wave = psi_all[s].astype(F32)
        norm = fold(wave * wave) if norm is None else norm + fold(wave * wave)
    norm_squared = jnp.sum(norm)

    total = own_block[...]
    for peer in peers:
        arrive(z_recv.at[peer], z_s.at[peer], z_r.at[peer], {"term": peer})
        total = total + z_recv[peer].astype(F32)
    out_ref[blk] = total.astype(BF16)
    for i, peer in enumerate((across, diagonal, sib)):
        push(out_ref.at[blk], out_ref.at[blk], out_s.at[i], out_r.at[i], {"blk": peer})

    for peer in peers:
        arrive(dots_recv.at[2 + peer], dot_s.at[2 + peer], dot_r.at[2 + peer], {"term": peer})
    dots_recv[2 + me] = dots[2]
    correlation = dots_recv[2]
    for z in range(1, n):
        correlation = correlation + dots_recv[2 + z]
    rayleigh_ref[...] = jnp.full(
        rayleigh_ref.shape, jnp.sum(correlation) / (norm_squared + 1e-06), F32
    )
    for i, peer in enumerate((across, diagonal, sib)):
        arrive(out_ref.at[peer], out_s.at[i], out_r.at[i], {"blk": peer})
    for copy in sends:
        copy.wait_send()


def fused(wavefunction, left_operator_table, op_right, term_source, term_target, n):
    sectors, rows, width = wavefunction.shape
    terms, slots = left_operator_table.shape[:2]
    block = (width, width)
    dma = pltpu.SemaphoreType.DMA
    vmem = pl.BlockSpec(memory_space=pltpu.VMEM)
    smem = pl.BlockSpec(memory_space=pltpu.SMEM)
    hbm = pl.BlockSpec(memory_space=pl.ANY)
    out, rayleigh = pl.pallas_call(
        functools.partial(kernel, n),
        out_shape=(
            jax.ShapeDtypeStruct((sectors, rows, width), BF16),
            jax.ShapeDtypeStruct((8, 128), F32),
        ),
        in_specs=[vmem, hbm, hbm, smem, smem],
        out_specs=(vmem, vmem),
        scratch_shapes=[
            pltpu.VMEM((sectors,) + block, BF16),
            pltpu.VMEM((terms, slots) + block, BF16),
            pltpu.VMEM((terms, slots) + block, BF16),
            pltpu.VMEM((terms, slots + 1) + block, BF16),
            pltpu.VMEM((2,) + block, F32),
            pltpu.VMEM((2,) + block, BF16),
            pltpu.VMEM((2,) + block, BF16),
            pltpu.VMEM(block, BF16),
            pltpu.VMEM(block, BF16),
            pltpu.VMEM((n - 1, rows, width), BF16),
            pltpu.VMEM((n, rows, width), BF16),
            pltpu.VMEM((rows, width), F32),
            pltpu.VMEM((3, 8, width), F32),
            pltpu.VMEM((2 + n, 8, width), F32),
            dma((2, terms)),
            dma((n,)), dma((n,)), dma((n,)), dma((n,)), dma((n,)), dma((n,)), dma((n,)), dma((n,)),
            dma((2,)), dma((2,)), dma((n,)), dma((n,)), dma((n,)), dma((n,)),
            dma((3,)), dma((3,)), dma((2 + n,)), dma((2 + n,)),
        ],
        compiler_params=pltpu.CompilerParams(
            collective_id=0, has_side_effects=True, vmem_limit_bytes=48 * 1024 * 1024
        ),
    )(wavefunction, left_operator_table, op_right, term_source, term_target)
    applied = out.astype(F32)
    return applied, applied - rayleigh[0, 0] * wavefunction.astype(F32)


def plain(wavefunction, left_operator_table, op_right, term_source, term_target):
    sectors = wavefunction.shape[0]
    block_width = wavefunction.shape[2]
    item_count = left_operator_table.shape[0] * left_operator_table.shape[1]
    left_operator_blocks = left_operator_table.reshape(item_count, block_width, block_width)
    right_blocks = op_right.reshape(item_count, block_width, block_width)
    source = term_source.reshape(item_count)
    target = term_target.reshape(item_count)
    whole_psi = lax.all_gather(wavefunction, "term", axis=1, tiled=True)
    selected_blocks = jnp.take(whole_psi, source, axis=0)
    half_products = jnp.einsum(
        "xwm,xmp->xwp", left_operator_blocks, selected_blocks, preferred_element_type=F32
    )
    half_products = half_products.astype(BF16)
    term_products = jnp.einsum(
        "iab,icb->iac", half_products, right_blocks, preferred_element_type=F32
    )
    onehot = (target[:, None] == jnp.arange(sectors, dtype=jnp.int32)[None, :]).astype(F32)
    partial_value = jnp.einsum(
        "is,iac->sac", onehot, term_products, precision=lax.Precision.HIGHEST
    )
    column_share = lax.psum_scatter(partial_value, "blk", scatter_dimension=2, tiled=True)
    both_share = lax.psum_scatter(column_share, "term", scatter_dimension=1, tiled=True)
    applied = lax.all_gather(both_share, "blk", axis=2, tiled=True)
    wave_float = wavefunction.astype(F32)
    correlation, norm_squared = lax.psum(
        (jnp.sum(wave_float * applied), jnp.sum(wave_float * wave_float)), "term"
    )
    rayleigh = correlation / (norm_squared + 1e-06)
    residual = applied - rayleigh * wave_float
    return (applied, residual)


def solution(mesh):
    n, groups = mesh.shape["term"], mesh.shape["blk"]

    def local(wavefunction, *rest):
        sectors, rows, _ = wavefunction.shape
        if groups == sectors == 4 and n == 4 and rows % 16 == 0:
            return fused(wavefunction, *rest, n)
        return plain(wavefunction, *rest)

    return jax.shard_map(
        local,
        mesh=mesh,
        in_specs=(
            P("parts", "term", None),
            P(("parts", "term", "blk"), None, None, None),
            P(("parts", "term", "blk"), None, None, None),
            P(("parts", "term", "blk"), None),
            P(("parts", "term", "blk"), None),
        ),
        out_specs=(P("parts", "term", None), P("parts", "term", None)),
        check_vma=False,
    )
```

time: 198 us -> 45 us (0.23); the launches traced: 195 us -> 44.8 us
  waiting for transfers between devices: 128 us -> 0 us
  Pallas kernels: 0 us -> 36.5 us
  blocking collectives: 17.9 us -> 0 us
  between operations: 16.4 us -> 0.65 us
  local copies, waits for them, and re-layouts: 18.8 us -> 5.86 us
  matrix products: 12 us -> 0 us
    unnamed x5 -> x0, waiting for transfers between devices: 96.6 us -> none
    pallas_call x0 -> x1, Pallas kernels: none -> 36.5 us  [fused(): pl.pallas_call(functools.partial(kernel, n), out_shape=(jax.ShapeDtypeStr...]
    all_gather x1 -> x0, waiting for transfers between devices: 31.3 us -> none  [local(): whole_psi = lax.all_gather(wavefunction, 'term', axis=1, tiled=True)]
    dot_general x2 -> x0, matrix products: 12 us -> none  [the longest x1 6.07 us: local(): jnp.einsum('is,iac->sac', onehot, term_products, precision=lax.Precision....]
    all_gather x1 -> x0, blocking collectives: 9.17 us -> none  [local(): applied = lax.all_gather(both_share, 'blk', axis=2, tiled=True)]
    psum x1 -> x0, blocking collectives: 8.72 us -> none  [local(): lax.psum((jnp.sum(wave_float * applied), jnp.sum(wave_float * wave_float)...]
    dot_general x1 -> x0, local copies, waits for them, and re-layouts: 5.59 us -> none  [local(): jnp.einsum('iab,icb->iac', half_products, right_blocks, preferred_element...]
    gather x1 -> x0, local copies, waits for them, and re-layouts: 2.22 us -> none  [local(): selected_blocks = jnp.take(whole_psi, source, axis=0)]
  transfers between devices with their start and end apart: 3 -> 0, of which waited for: 3 -> 0; matrix products, arithmetic and copies ran while one was open for 2% -> 0% of each run, Pallas kernels for 0% -> 0%
where the time goes in v1:
time: 45 us; the launch traced here: 44.8 us
  Pallas kernels  36.5 us (81%)
  local copies, waits for them, and re-layouts  5.86 us (13%)
  other arithmetic  1.78 us (4%)
  between operations  0.65 us (1%)
    pallas_call x1, Pallas kernels, fused(): pl.pallas_call(functools.partial(kernel, n), out_shape=(jax.ShapeDtypeStr...  36.5 us
    unnamed x10, local copies, waits for them, and re-layouts  5.26 us
    sub x1, other arithmetic, fused(): return (applied, applied - rayleigh[0, 0] * wavefunction.astype(F32))  1.78 us

profile of v1, /device:TPU:1, one launch (start us, length us, event | category | flops | bytes accessed | tf_op | source)
XLA Modules:
  0.0 44.8 jit_solution(14636861181384107764)
XLA Ops:
  0.6 0.0 copy-start
  0.6 1.5 %copy-done = bf16[2,3,384,384]{3,2,1,0:T(8,128)(2,1)S(1)} copy-done((bf16[2,3,384,384]{3,2,1,0:T(8,128)(2,1)S(1)}, bf16[2,3,384,384]{3,2,1,0:T(8,128)(2,1)}, u32[]{:S(2)}) %copy-start) | copy-done | bytes 1769496
  2.1 0.0 copy-start.1
  2.1 1.5 %copy-done.1 = bf16[2,3,384,384]{3,2,1,0:T(8,128)(2,1)S(1)} copy-done((bf16[2,3,384,384]{3,2,1,0:T(8,128)(2,1)S(1)}, bf16[2,3,384,384]{3,2,1,0:T(8,128)(2,1)}, u32[]{:S(2)}) %copy-start.1) | copy-done | bytes 1769496
  3.6 0.0 copy-start.2
  3.6 1.0 %copy-done.2 = bf16[4,96,384]{2,1,0:T(8,128)(2,1)S(1)} copy-done((bf16[4,96,384]{2,1,0:T(8,128)(2,1)S(1)}, bf16[4,96,384]{2,1,0:T(8,128)(2,1)}, u32[]{:S(2)}) %copy-start.2) | copy-done | bytes 294936
  4.5 0.0 copy-start.3
  4.5 0.7 %copy-done.3 = s32[2,3]{1,0:T(2,128)S(1)} copy-done((s32[2,3]{1,0:T(2,128)S(1)}, s32[2,3]{1,0:T(2,128)}, u32[]{:S(2)}) %copy-start.3) | copy-done | bytes 48
  5.2 0.0 copy-start.4
  5.2 0.7 %copy-done.4 = s32[2,3]{1,0:T(2,128)S(1)} copy-done((s32[2,3]{1,0:T(2,128)S(1)}, s32[2,3]{1,0:T(2,128)}, u32[]{:S(2)}) %copy-start.4) | copy-done | bytes 48
  5.9 36.5 %shard_map.68 = (bf16[4,96,384]{2,1,0:T(8,128)(2,1)S(1)}, f32[8,128]{1,0:T(8,128)S(1)}) custom-call(bf16[4,96,384]{2,1,0:T(8,128)(2,1)S(1)} %copy-done.2, bf16[2,3,384,384]{3,2,1,0:T(8,128)(2,1)S(1)} %copy-done, bf16[2,3,384,384]{3,2,1,0:T(8,128)(2,1)S(1)} %copy-done.1, s32[2,3]{1,0:T(2,128)S(1)} %copy-done.3, s32[2,3]{1,0:T(2,128)S(1)} %copy-done.4), custom_call_target="tpu_custom_call" | custom-call | tf_op jit(solution)/shard_map/pallas_call | solution.py:196
  42.4 0.6 %slice.3 = f32[1,1]{1,0:T(1,128)} slice(f32[8,128]{1,0:T(8,128)S(1)} %get-tuple-element.5), slice={[0:1], [0:1]} | slice | bytes 8 | tf_op jit(solution)/shard_map/slice | solution.py:229
  43.0 1.8 %multiply_subtract_fusion = (f32[4,96,384]{2,1,0:T(8,128)}, f32[4,96,384]{2,1,0:T(8,128)}) fusion(bf16[4,96,384]{2,1,0:T(8,128)(2,1)S(1)} %copy-done.2, f32[]{:T(128)} %bitcast, bf16[4,96,384]{2,1,0:T(8,128)(2,1)S(1)} %get-tuple-element.4), kind=kLoop, calls=%fused_computation | loop fusion | flops 589824 | bytes 1769476 | tf_op jit(solution)/shard_map/sub | solution.py:229
Async XLA Ops:
  0.6 1.5 %copy-start = (bf16[2,3,384,384]{3,2,1,0:T(8,128)(2,1)S(1)}, bf16[2,3,384,384]{3,2,1,0:T(8,128)(2,1)}, u32[]{:S(2)}) copy-start(bf16[2,3,384,384]{3,2,1,0:T(8,128)(2,1)} %left_hbm.1) | copy-start | bytes 5308420
  2.1 1.5 %copy-start.1 = (bf16[2,3,384,384]{3,2,1,0:T(8,128)(2,1)S(1)}, bf16[2,3,384,384]{3,2,1,0:T(8,128)(2,1)}, u32[]{:S(2)}) copy-start(bf16[2,3,384,384]{3,2,1,0:T(8,128)(2,1)} %right_hbm.1) | copy-start | bytes 5308420
  3.6 1.0 %copy-start.2 = (bf16[4,96,384]{2,1,0:T(8,128)(2,1)S(1)}, bf16[4,96,384]{2,1,0:T(8,128)(2,1)}, u32[]{:S(2)}) copy-start(bf16[4,96,384]{2,1,0:T(8,128)(2,1)} %psi_ref.1) | copy-start | bytes 884740
  4.5 0.7 %copy-start.3 = (s32[2,3]{1,0:T(2,128)S(1)}, s32[2,3]{1,0:T(2,128)}, u32[]{:S(2)}) copy-start(s32[2,3]{1,0:T(2,128)} %source_ref.1) | copy-start | bytes 76
  5.2 0.7 %copy-start.4 = (s32[2,3]{1,0:T(2,128)S(1)}, s32[2,3]{1,0:T(2,128)}, u32[]{:S(2)}) copy-start(s32[2,3]{1,0:T(2,128)} %target_ref.1) | copy-start | bytes 76

commit v2 on v1

--- a/solution.py
+++ b/solution.py
@@ -22,7 +22,7 @@
     out_ref, rayleigh_ref,
     psi_all, left, right, half, kept, pair_send, pair_recv, x_send, x_recv, z_send, z_recv,
     own_block, dots, dots_recv,
-    load_sem, gz_s, gz_r, gx_s, gx_r, gc_s, gc_r, gd_s, gd_r,
+    own_sem, load_sem, gz_s, gz_r, gx_s, gx_r, gc_s, gc_r,
     pair_s, pair_r, x_s, x_r, z_s, z_r, out_s, out_r, dot_s, dot_r,
 ):
     terms, slots = left.shape[0], left.shape[1]
@@ -39,6 +39,8 @@
     for t in range(terms):
         loads.append(pltpu.make_async_copy(left_hbm.at[t], left.at[t], load_sem.at[0, t]))
         loads.append(pltpu.make_async_copy(right_hbm.at[t], right.at[t], load_sem.at[1, t]))
+    own_rows = pltpu.make_async_copy(psi_ref, psi_all.at[:, pl.ds(pl.multiple_of(me * rows, rows), rows)], own_sem)
+    own_rows.start()
     for load in loads:
         load.start()
 
@@ -74,27 +76,50 @@
     def span(z):
         return pl.ds(pl.multiple_of(z * rows, rows), rows)
 
-    for peer in peers:
-        push(psi_ref.at[blk], psi_all.at[blk, span(me)], gz_s.at[peer], gz_r.at[me], {"term": peer})
-    for s in range(psi_ref.shape[0]):
-        psi_all[s, span(me)] = psi_ref[s]
-
-    for peer in peers:
-        piece = psi_all.at[blk, span(peer)]
-        arrive(piece, gz_s.at[peer], gz_r.at[peer], {"term": peer})
+    crossing = rows * 2 // 3 // 16 * 16
+
+    def upper(z):
+        return pl.ds(pl.multiple_of(z * rows, 16), crossing)
+
+    def lower(z):
+        return pl.ds(pl.multiple_of(z * rows + crossing, 16), rows - crossing)
+
+    def straight():
+        for peer in peers:
+            for i, s in enumerate((blk, across)):
+                push(psi_ref.at[s, pl.ds(crossing, rows - crossing)], psi_all.at[s, lower(me)],
+                     gz_s.at[1 + i, peer], gz_r.at[1 + i, me], {"term": peer})
+
+    for peer in peers:
+        push(psi_ref.at[blk, pl.ds(0, crossing)], psi_all.at[blk, upper(me)],
+             gz_s.at[0, peer], gz_r.at[0, me], {"term": peer})
+    for i, peer in enumerate(peers):
+        piece = psi_all.at[blk, upper(peer)]
+        arrive(piece, gz_s.at[0, peer], gz_r.at[0, peer], {"term": peer})
         push(piece, piece, gx_s.at[peer], gx_r.at[peer], {"blk": across})
-        push(piece, piece, gc_s.at[peer], gc_r.at[peer], {"blk": sib})
-    for peer in peers:
-        piece = psi_all.at[across, span(peer)]
+        if i == 0:
+            straight()
+        push(piece, piece, gc_s.at[0, peer], gc_r.at[0, peer], {"blk": sib})
+    for peer in peers:
+        for i, s in enumerate((blk, across)):
+            piece = psi_all.at[s, lower(peer)]
+            arrive(piece, gz_s.at[1 + i, peer], gz_r.at[1 + i, peer], {"term": peer})
+            push(piece, piece, gc_s.at[1 + i, peer], gc_r.at[1 + i, peer], {"blk": sib})
+    for peer in peers:
+        piece = psi_all.at[across, upper(peer)]
         arrive(piece, gx_s.at[peer], gx_r.at[peer], {"blk": across})
-        push(piece, piece, gd_s.at[peer], gd_r.at[peer], {"blk": sib})
+        push(piece, piece, gc_s.at[3, peer], gc_r.at[3, peer], {"blk": sib})
     for t in range(terms):
         half[t, slots] = jnp.zeros(half.shape[2:], BF16)
+    own_rows.wait()
     for load in loads:
         load.wait()
     for peer in peers:
-        arrive(psi_all.at[sib, span(peer)], gc_s.at[peer], gc_r.at[peer], {"blk": sib})
-        arrive(psi_all.at[diagonal, span(peer)], gd_s.at[peer], gd_r.at[peer], {"blk": sib})
+        for i, piece in enumerate((
+            psi_all.at[sib, upper(peer)], psi_all.at[sib, lower(peer)],
+            psi_all.at[diagonal, lower(peer)], psi_all.at[diagonal, upper(peer)],
+        )):
+            arrive(piece, gc_s.at[i, peer], gc_r.at[i, peer], {"blk": sib})
 
     for t in range(terms):
         for k in range(slots):
@@ -197,9 +222,9 @@
         functools.partial(kernel, n),
         out_shape=(
             jax.ShapeDtypeStruct((sectors, rows, width), BF16),
-            jax.ShapeDtypeStruct((8, 128), F32),
+            jax.ShapeDtypeStruct((rows, width), F32),
         ),
-        in_specs=[vmem, hbm, hbm, smem, smem],
+        in_specs=[hbm, hbm, hbm, smem, smem],
         out_specs=(vmem, vmem),
         scratch_shapes=[
             pltpu.VMEM((sectors,) + block, BF16),
@@ -216,17 +241,17 @@
             pltpu.VMEM((rows, width), F32),
             pltpu.VMEM((3, 8, width), F32),
             pltpu.VMEM((2 + n, 8, width), F32),
-            dma((2, terms)),
-            dma((n,)), dma((n,)), dma((n,)), dma((n,)), dma((n,)), dma((n,)), dma((n,)), dma((n,)),
+            dma, dma((2, terms)),
+            dma((3, n)), dma((3, n)), dma((n,)), dma((n,)), dma((4, n)), dma((4, n)),
             dma((2,)), dma((2,)), dma((n,)), dma((n,)), dma((n,)), dma((n,)),
             dma((3,)), dma((3,)), dma((2 + n,)), dma((2 + n,)),
         ],
         compiler_params=pltpu.CompilerParams(
-            collective_id=0, has_side_effects=True, vmem_limit_bytes=48 * 1024 * 1024
+            collective_id=0, has_side_effects=True, vmem_limit_bytes=60 * 1024 * 1024
         ),
     )(wavefunction, left_operator_table, op_right, term_source, term_target)
     applied = out.astype(F32)
-    return applied, applied - rayleigh[0, 0] * wavefunction.astype(F32)
+    return applied, applied - rayleigh * wavefunction.astype(F32)
 
 
 def plain(wavefunction, left_operator_table, op_right, term_source, term_target):

time: 45 us -> 38.5 us (0.86)
  local copies, waits for them, and re-layouts: 5.86 us -> 0.01 us
  Pallas kernels: 36.5 us -> 35.5 us
    unnamed x10 -> x2, local copies, waits for them, and re-layouts: 5.26 us -> 0.01 us
    pallas_call x1, Pallas kernels: 36.5 us -> 35.5 us  [fused(): pl.pallas_call(functools.partial(kernel, n), out_shape=(jax.ShapeDtypeStr...]
    slice x1 -> x0, local copies, waits for them, and re-layouts: 0.59 us -> none  [fused(): return (applied, applied - rayleigh[0, 0] * wavefunction.astype(F32))]
where the time goes in v2:
time: 38.5 us; the launch traced here: 38.3 us
  Pallas kernels  35.5 us (92%)
  other arithmetic  2.13 us (6%)
  between operations  0.65 us (2%)
    pallas_call x1, Pallas kernels, fused(): pl.pallas_call(functools.partial(kernel, n), out_shape=(jax.ShapeDtypeStr...  35.5 us
    sub x1, other arithmetic, fused(): return (applied, applied - rayleigh * wavefunction.astype(F32))  2.13 us

profile of v2, /device:TPU:1, one launch (start us, length us, event | category | flops | bytes accessed | tf_op | source)
XLA Modules:
  0.0 38.3 jit_solution(8014359005532084849)
XLA Ops:
  0.6 0.0 copy-start
  0.6 35.5 %shard_map.68 = (bf16[4,96,384]{2,1,0:T(8,128)(2,1)}, f32[96,384]{1,0:T(8,128)}) custom-call(bf16[4,96,384]{2,1,0:T(8,128)(2,1)} %psi_ref.1, bf16[2,3,384,384]{3,2,1,0:T(8,128)(2,1)} %left_hbm.1, bf16[2,3,384,384]{3,2,1,0:T(8,128)(2,1)} %right_hbm.1, s32[2,3]{1,0:T(2,128)} %source_ref.1, s32[2,3]{1,0:T(2,128)} %target_ref.1), custom_call_target="tpu_custom_call" | custom-call | tf_op jit(solution)/shard_map/pallas_call | solution.py:221
  36.1 0.0 copy-done
  36.2 2.1 %multiply_subtract_fusion = (f32[4,96,384]{2,1,0:T(8,128)}, f32[4,96,384]{2,1,0:T(8,128)}) fusion(bf16[4,96,384]{2,1,0:T(8,128)(2,1)S(1)} %copy-done, f32[96,384]{1,0:T(8,128)} %get-tuple-element.5, bf16[4,96,384]{2,1,0:T(8,128)(2,1)} %get-tuple-element.4), kind=kLoop, calls=%fused_computation | loop fusion | flops 589824 | bytes 1916928 | tf_op jit(solution)/shard_map/sub | solution.py:254
Async XLA Ops:
  0.6 35.5 %copy-start = (bf16[4,96,384]{2,1,0:T(8,128)(2,1)S(1)}, bf16[4,96,384]{2,1,0:T(8,128)(2,1)}, u32[]{:S(2)}) copy-start(bf16[4,96,384]{2,1,0:T(8,128)(2,1)} %psi_ref.1) | copy-start | bytes 884740

commit v3 on v2

--- a/solution.py
+++ b/solution.py
@@ -127,40 +127,57 @@
                 left[t, k], psi_all[source_ref[t, k]], preferred_element_type=F32
             ).astype(BF16)
 
-    def partial(s):
+    width = psi_ref.shape[2]
+    middle = width // 2 // 16 * 16
+
+    def partial(s, low=0, high=width):
         total = None
         for t in range(terms):
             k = slots
             for slot in range(slots):
                 k = jnp.where(target_ref[t, slot] == s, slot, k)
             product = lax.dot_general(
-                half[t, k], right[t, jnp.minimum(k, slots - 1)],
+                half[t, k, low:high], right[t, jnp.minimum(k, slots - 1)],
                 (((1,), (1,)), ((), ())), preferred_element_type=F32,
             )
             total = product if total is None else total + product
-        return total, fold(psi_all[s].astype(F32) * total)
+        return total
 
     far = peers[::-1]
     order = far + [me]
 
-    value, dot = partial(diagonal)
-    pair_send[0] = value.astype(BF16)
-    push(pair_send.at[0], pair_recv.at[0], pair_s.at[0], pair_r.at[0], {"blk": sib})
-    value, more = partial(across)
-    dot = dot + more
-    kept[0] = value
-    arrive(pair_recv.at[0], pair_s.at[0], pair_r.at[0], {"blk": sib})
-    for z in order:
+    def cross(z):
         x_send[span(z)] = (kept[0, span(z)] + pair_recv[0, span(z)].astype(F32)).astype(BF16)
         push(x_send.at[span(z)], x_recv.at[span(z)], x_s.at[z], x_r.at[z], {"blk": across})
-    value, more = partial(sib)
-    dot = dot + more
+
+    cuts = ((0, 0, middle), (2, middle, width))
+    for i, low, high in cuts:
+        value = partial(diagonal, low, high)
+        pair_send[0, low:high] = value.astype(BF16)
+        piece = pl.ds(low, high - low)
+        push(pair_send.at[0, piece], pair_recv.at[0, piece], pair_s.at[i], pair_r.at[i], {"blk": sib})
+        kept[2, low:high] = value
+    kept[0] = partial(across)
+    for i, low, high in cuts:
+        arrive(pair_recv.at[0, pl.ds(low, high - low)], pair_s.at[i], pair_r.at[i], {"blk": sib})
+    for z in order[:2]:
+        cross(z)
+    value = partial(sib)
     pair_send[1] = value.astype(BF16)
     push(pair_send.at[1], pair_recv.at[1], pair_s.at[1], pair_r.at[1], {"blk": sib})
-    value, more = partial(blk)
-    dots[0] = dot + more
+    kept[3] = value
+    for z in order[2:3]:
+        cross(z)
+    kept[1] = partial(blk)
+    for z in order[3:4]:
+        cross(z)
+    dot = fold(psi_all[diagonal].astype(F32) * kept[2])
+    for i, s in ((0, across), (3, sib), (1, blk)):
+        dot = dot + fold(psi_all[s].astype(F32) * kept[i])
+    for z in order[4:]:
+        cross(z)
+    dots[0] = dot
     push(dots.at[0], dots_recv.at[0], dot_s.at[0], dot_r.at[0], {"blk": sib})
-    kept[1] = value
     arrive(pair_recv.at[1], pair_s.at[1], pair_r.at[1], {"blk": sib})
 
     for i, z in enumerate(order):
@@ -231,7 +248,7 @@
             pltpu.VMEM((terms, slots) + block, BF16),
             pltpu.VMEM((terms, slots) + block, BF16),
             pltpu.VMEM((terms, slots + 1) + block, BF16),
-            pltpu.VMEM((2,) + block, F32),
+            pltpu.VMEM((4,) + block, F32),
             pltpu.VMEM((2,) + block, BF16),
             pltpu.VMEM((2,) + block, BF16),
             pltpu.VMEM(block, BF16),
@@ -243,7 +260,7 @@
             pltpu.VMEM((2 + n, 8, width), F32),
             dma, dma((2, terms)),
             dma((3, n)), dma((3, n)), dma((n,)), dma((n,)), dma((4, n)), dma((4, n)),
-            dma((2,)), dma((2,)), dma((n,)), dma((n,)), dma((n,)), dma((n,)),
+            dma((3,)), dma((3,)), dma((n,)), dma((n,)), dma((n,)), dma((n,)),
             dma((3,)), dma((3,)), dma((2 + n,)), dma((2 + n,)),
         ],
         compiler_params=pltpu.CompilerParams(

time: 38.5 us -> 38.8 us (level)
  Pallas kernels: 35.5 us -> 35.9 us
where the time goes in v3:
time: 38.8 us; the launch traced here: 38.7 us
  Pallas kernels  35.9 us (93%)
  other arithmetic  2.13 us (5%)
  between operations  0.65 us (2%)
    pallas_call x1, Pallas kernels, fused(): pl.pallas_call(functools.partial(kernel, n), out_shape=(jax.ShapeDtypeStr...  35.9 us
    sub x1, other arithmetic, fused(): return (applied, applied - rayleigh * wavefunction.astype(F32))  2.13 us

profile of v3, /device:TPU:1, one launch (start us, length us, event | category | flops | bytes accessed | tf_op | source)
XLA Modules:
  0.0 38.7 jit_solution(15999685406344335119)
XLA Ops:
  0.6 0.0 copy-start
  0.6 35.9 %shard_map.68 = (bf16[4,96,384]{2,1,0:T(8,128)(2,1)}, f32[96,384]{1,0:T(8,128)}) custom-call(bf16[4,96,384]{2,1,0:T(8,128)(2,1)} %psi_ref.1, bf16[2,3,384,384]{3,2,1,0:T(8,128)(2,1)} %left_hbm.1, bf16[2,3,384,384]{3,2,1,0:T(8,128)(2,1)} %right_hbm.1, s32[2,3]{1,0:T(2,128)} %source_ref.1, s32[2,3]{1,0:T(2,128)} %target_ref.1), custom_call_target="tpu_custom_call" | custom-call | tf_op jit(solution)/shard_map/pallas_call | solution.py:238
  36.5 0.0 copy-done
  36.5 2.1 %multiply_subtract_fusion = (f32[4,96,384]{2,1,0:T(8,128)}, f32[4,96,384]{2,1,0:T(8,128)}) fusion(bf16[4,96,384]{2,1,0:T(8,128)(2,1)S(1)} %copy-done, f32[96,384]{1,0:T(8,128)} %get-tuple-element.5, bf16[4,96,384]{2,1,0:T(8,128)(2,1)} %get-tuple-element.4), kind=kLoop, calls=%fused_computation | loop fusion | flops 589824 | bytes 1916928 | tf_op jit(solution)/shard_map/sub | solution.py:271
Async XLA Ops:
  0.6 35.9 %copy-start = (bf16[4,96,384]{2,1,0:T(8,128)(2,1)S(1)}, bf16[4,96,384]{2,1,0:T(8,128)(2,1)}, u32[]{:S(2)}) copy-start(bf16[4,96,384]{2,1,0:T(8,128)(2,1)} %psi_ref.1) | copy-start | bytes 884740
